TPU v7x, 32 devices: a whole 2x2x4 slice. The times are simulated.
32 devices in a mesh: parts: 2 (over x), wave: 8 (over z, y), pos: 2 (over core).
Axes of the slice: x: 2, y: 2, z: 4, core: 2. Of those that a mesh axis runs over, the one named last changes fastest.
Arguments:
- object_field: float32 [2, 1536, 768], P(None, 'parts'), parts along dimension 1, may hold values from -4 to 4
- probe_field: float32 [8, 2, 1024, 512], P('wave', None, 'parts'), parts along dimension 2, may hold values from -4.5 to 4.5
- resample_blocks: bfloat16 [8, 8, 64, 128], P('wave'), may hold values from -0.5 to 0.5
- band_start: int32 [8, 8], P('wave'), may hold values from 0 to 6
- measured_amplitude: bfloat16 [2, 1024, 512], P('pos', 'parts'), parts along dimension 1, may hold values from 0 to 3.1875
- patch_offsets: int32 [4, 2], P('parts', 'pos'), parts along dimension 0, may hold values from 0 to 256
Outputs:
- object_grad: float32 [2, 1536, 768], P(None, ('parts', 'wave', 'pos')), parts along dimension 1
- probe_grad: float32 [8, 2, 1024, 512], P('wave', None, 'parts'), parts along dimension 2
There are 2 independent parts, one for each index of `parts`. A program takes and returns all parts, laid end to end along the dimension named above; an argument that names none is the same for every part. Nothing has to cross between parts.
All inputs are finite; a program needn't handle non-finite values.
Results may differ from a plain program's by a relative error of at most 0.013.
Values sent between devices are 32-bit elements; how exact they have to be, the bound alone decides.
A program may use at most 128 MiB of HBM per device.

v0:
```python
import math

import jax
import jax.numpy as jnp
from jax import lax
from jax.sharding import PartitionSpec as P


def dft_table(length, flip_sign):
    index_line = jnp.arange(length, dtype=jnp.int32)
    phase_steps = index_line[:, None] * index_line[None, :] % length
    angles = phase_steps.astype(jnp.float32) * (2.0 * math.pi / length)
    scaling = 1.0 / math.sqrt(length)
    real_part = jnp.cos(angles) * scaling
    imag_part = flip_sign * jnp.sin(angles) * scaling
    matrix = jnp.stack([jnp.stack([real_part, -imag_part]), jnp.stack([imag_part, real_part])])
    return matrix.astype(jnp.bfloat16)


def band_picker(starts, band_count, block_count):
    band_steps = jnp.arange(band_count, dtype=jnp.int32)
    targets = starts[:, None] + band_steps[None, :]
    columns = jnp.arange(block_count, dtype=jnp.int32)
    return (targets[:, :, None] == columns[None, None, :]).astype(jnp.float32)


def complex_left(matrix, values):
    return jnp.einsum("dcxm,pcmy->pdxy", matrix, values, preferred_element_type=jnp.float32)


def complex_right(values, matrix):
    return jnp.einsum("pcxm,dcmy->pdxy", values, matrix, preferred_element_type=jnp.float32)


def exit_wave(probe_wave, patches):
    real_part = probe_wave[0] * patches[:, 0] - probe_wave[1] * patches[:, 1]
    imag_part = probe_wave[0] * patches[:, 1] + probe_wave[1] * patches[:, 0]
    return jnp.stack([real_part, imag_part], axis=1).astype(jnp.bfloat16)


def forward_pass(exit_field, forward_matrix, blocks, picker):
    positions_here = exit_field.shape[0]
    patch_side = exit_field.shape[2]
    block_count, block_rows, band_width = blocks.shape
    far_blocks = picker.shape[2]
    detector_side = block_count * block_rows
    pick_low = picker.astype(jnp.bfloat16)
    half_step = complex_left(forward_matrix, exit_field).astype(jnp.bfloat16)
    far_field = complex_right(half_step, forward_matrix).astype(jnp.bfloat16)
    grouped = far_field.reshape(positions_here, 2, far_blocks, block_rows, patch_side)
    chosen = jnp.einsum(
        "ktn,pcnbx->pcktbx", pick_low, grouped, preferred_element_type=jnp.float32
    ).astype(jnp.bfloat16)
    chosen = chosen.reshape(positions_here, 2, block_count, band_width, patch_side)
    resampled = jnp.einsum(
        "kbr,pckrx->pckbx", blocks, chosen, preferred_element_type=jnp.float32
    ).astype(jnp.bfloat16)
    split_cols = resampled.reshape(positions_here, 2, detector_side, far_blocks, block_rows)
    chosen_cols = jnp.einsum(
        "ktn,pcxnb->pcxktb", pick_low, split_cols, preferred_element_type=jnp.float32
    ).astype(jnp.bfloat16)
    chosen_cols = chosen_cols.reshape(positions_here, 2, detector_side, block_count, band_width)
    detector_field = jnp.einsum(
        "pcxkr,kbr->pcxkb", chosen_cols, blocks, preferred_element_type=jnp.float32
    )
    return detector_field.reshape(positions_here, 2, detector_side, detector_side)


def backward_pass(detector_grad, inverse_matrix, blocks, picker):
    positions_here = detector_grad.shape[0]
    block_count, block_rows, band_width = blocks.shape
    band_count = picker.shape[1]
    far_blocks = picker.shape[2]
    detector_side = block_count * block_rows
    patch_side = far_blocks * block_rows
    split_cols = detector_grad.reshape(positions_here, 2, detector_side, block_count, block_rows)
    spread = jnp.einsum("pcxkb,kbr->pcxkr", split_cols, blocks, preferred_element_type=jnp.float32)
    spread = spread.reshape(positions_here, 2, detector_side, block_count, band_count, block_rows)
    row_grad = jnp.einsum(
        "pcxktb,ktn->pcxnb", spread, picker, precision=lax.Precision.HIGHEST
    ).astype(jnp.bfloat16)
    split_rows = row_grad.reshape(positions_here, 2, block_count, block_rows, patch_side)
    lifted = jnp.einsum("kbr,pckbx->pckrx", blocks, split_rows, preferred_element_type=jnp.float32)
    lifted = lifted.reshape(positions_here, 2, block_count, band_count, block_rows, patch_side)
    far_grad = jnp.einsum(
        "pcktbx,ktn->pcnbx", lifted, picker, precision=lax.Precision.HIGHEST
    ).astype(jnp.bfloat16)
    far_grad = far_grad.reshape(positions_here, 2, patch_side, patch_side)
    half_grad = complex_right(far_grad, inverse_matrix).astype(jnp.bfloat16)
    return complex_left(inverse_matrix, half_grad)


def patch_corner(patch_offsets, position):
    zero_index = jnp.zeros((), jnp.int32)
    return (zero_index, patch_offsets[0, position], patch_offsets[1, position])


def local(
    object_field, probe_field, resample_blocks, band_start, measured_amplitude, patch_offsets
):
    waves_here = probe_field.shape[0]
    waves_total = waves_here * lax.axis_size("wave")
    patch_side = probe_field.shape[2]
    object_side = object_field.shape[1]
    block_rows = resample_blocks.shape[2]
    band_count = resample_blocks.shape[3] // block_rows
    forward_matrix = dft_table(patch_side, -1.0)
    inverse_matrix = dft_table(patch_side, 1.0)
    corners = [patch_corner(patch_offsets, 0)]
    patches = jnp.stack(
        [lax.dynamic_slice(object_field, corner, (2, patch_side, patch_side)) for corner in corners]
    )
    wave_slot = 0
    picker = band_picker(band_start[wave_slot], band_count, patch_side // block_rows)
    exit_field = exit_wave(probe_field[wave_slot], patches)
    detector_field = forward_pass(exit_field, forward_matrix, resample_blocks[wave_slot], picker)
    fields = [detector_field]
    pickers = [picker]
    intensity_sum = jnp.sum(detector_field * detector_field, axis=1)
    intensity_all = lax.psum(intensity_sum, "wave")
    factor = 1.0 - measured_amplitude.astype(jnp.float32) / jnp.sqrt(
        intensity_all / waves_total + 1.0
    )
    wave_slot = 0
    probe_wave = probe_field[wave_slot]
    detector_grad = (factor[:, None] * fields[wave_slot]).astype(jnp.bfloat16)
    exit_grad = backward_pass(
        detector_grad, inverse_matrix, resample_blocks[wave_slot], pickers[wave_slot]
    )
    patch_real = probe_wave[0] * exit_grad[:, 0] + probe_wave[1] * exit_grad[:, 1]
    patch_imag = probe_wave[0] * exit_grad[:, 1] - probe_wave[1] * exit_grad[:, 0]
    patch_total = jnp.stack([patch_real, patch_imag], axis=1)
    probe_real = jnp.sum(patches[:, 0] * exit_grad[:, 0] + patches[:, 1] * exit_grad[:, 1], axis=0)
    probe_imag = jnp.sum(patches[:, 0] * exit_grad[:, 1] - patches[:, 1] * exit_grad[:, 0], axis=0)
    probe_terms = [jnp.stack([probe_real, probe_imag])]
    probe_grad = lax.psum(jnp.stack(probe_terms), "pos")
    patch_total = patch_total / waves_total
    object_local = jnp.zeros((2, object_side, object_side), jnp.float32)
    object_local = lax.dynamic_update_slice(object_local, patch_total[0], corners[0])
    object_grad = lax.psum_scatter(object_local, ("wave", "pos"), scatter_dimension=1, tiled=True)
    return (object_grad, probe_grad)


def solution(mesh):
    in_specs = (
        P(None, "parts", None),
        P("wave", None, "parts", None),
        P("wave", None, None, None),
        P("wave", None),
        P("pos", "parts", None),
        P("parts", "pos"),
    )
    out_specs = (P(None, ("parts", "wave", "pos"), None), P("wave", None, "parts", None))
    return jax.shard_map(local, mesh=mesh, in_specs=in_specs, out_specs=out_specs, check_vma=False)
```

profile of v0, /device:TPU:0, one launch (start us, length us, event | category | flops | bytes accessed | tf_op | source)
XLA Modules:
  0.0 288.9 jit_solution(17438887458617481917)
XLA Ops:
  7.2 0.0 copy-start
  7.2 0.0 copy-start.12
  7.2 0.0 all-reduce.3.cloned.1.call-start
  7.2 1.3 fusion.69
  11.1 4.6 %multiply_convert_fusion.2 = bf16[1,512,512]{2,1,0:T(8,128)(2,1)} fusion(), kind=kLoop, calls=%fused_computation.67 | loop fusion | flops 4194304 | bytes 524288 | tf_op jit(solution)/shard_map/convert.15
  15.8 5.4 %multiply_convert_fusion = (bf16[1,512,512]{2,1,0:T(8,128)(2,1)}, bf16[1,512,512]{2,1,0:T(8,128)(2,1)}) fusion(), kind=kLoop, calls=%fused_computation.62 | loop fusion | flops 4718592 | bytes 1048576 | tf_op jit(solution)/shard_map/convert.18
  21.2 4.7 %negate_convert_fusion = (bf16[1,512,512]{2,1,0:T(8,128)(2,1)}, bf16[1,512,512]{2,1,0:T(8,128)(2,1)}) fusion(), kind=kLoop, calls=%fused_computation.60 | loop fusion | flops 5242880 | bytes 1048576 | tf_op jit(solution)/shard_map/convert.11
  25.9 0.0 copy-done.12
  27.2 3.7 %constant_dynamic-slice_fusion = f32[2,512,512]{2,1,0:T(8,128)} fusion(f32[2,768,768]{2,1,0:T(8,128)} %param.6, s32[]{:T(128)S(6)} %select_n.55, s32[]{:T(128)S(6)} %select_n.56), kind=kLoop, calls=%fused_computation.84 | loop fusion | bytes 4194312 | tf_op jit(solution)/shard_map/dynamic_slice | solution.py:111
  30.9 1.9 copy.23
  32.8 3.1 %fusion.68 = (f32[1,1,512,512]{3,2,1,0:T(8,128)}, f32[1,1,512,512]{3,2,1,0:T(8,128)}) fusion(f32[1,2,512,512]{3,2,1,0:T(8,128)} %param.7), kind=kLoop, calls=%fused_computation.88 | loop fusion | bytes 4194304 | tf_op jit(solution)/shard_map/slice | solution.py:130
  35.9 1.6 copy.66
  37.4 2.5 copy.67
  40.0 0.0 copy-start.9
  40.0 3.0 %fusion.47 = (bf16[1,512,512]{1,2,0:T(8,128)(2,1)}, bf16[1,512,512]{1,2,0:T(8,128)(2,1)}) fusion(f32[1,1,512,512]{2,3,1,0:T(8,128)} %copy.67, f32[1,2,512,512]{2,3,1,0:T(8,128)S(1)} %bitcast.176, f32[1,1,512,512]{2,3,1,0:T(8,128)S(1)} %copy.66), kind=kLoop, calls=%fused_computation.68 | loop fusion | flops 2097152 | bytes 5242880 | tf_op jit(solution)/shard_map/stack | solution.py:38
  43.0 0.0 copy-done.5
  43.0 0.0 copy-done.6
  43.0 0.0 copy-done.7
  43.0 0.0 copy-done.8
  43.0 2.1 fusion.30
  45.1 5.8 %bitcast_convert_fusion.3 = bf16[2,512,512]{1,2,0:T(8,128)(2,1)} fusion(bf16[1,2,512,512]{3,2,1,0:T(8,128)(2,1)} %get-tuple-element.17, bf16[1,2,512,512]{3,2,1,0:T(8,128)(2,1)} %get-tuple-element.18, bf16[1,512,512]{1,2,0:T(8,128)(2,1)} %get-tuple-element.11, bf16[1,512,512]{1,2,0:T(8,128)(2,1)} %get-tuple-element.10), kind=kOutput, calls=%fused_computation.17 | convolution fusion | flops 2155872256 | bytes 4194304 | tf_op jit(solution)/shard_map/pcxm,dcmy->pdxy/dot_general | solution.py:32
  50.9 2.1 convert_bitcast_fusion.1
  53.1 1.2 copy.28
  54.2 0.4 fusion.17
  54.7 1.1 copy.30
  55.7 3.9 %reshape.398 = bf16[2,512,8,64]{3,2,1,0:T(8,128)(2,1)} reshape(bf16[1,2,8,64,512]{4,3,2,1,0:T(8,128)(2,1)} %copy.30) | data formatting | bytes 2097152 | tf_op jit(solution)/shard_map/reshape.20
  59.6 4.2 %copy.49 = bf16[2,512,8,64,1]{1,2,4,3,0:T(8,128)(2,1)} copy(bf16[2,512,8,64,1]{3,2,1,0,4:T(8,128)(2,1)} %bitcast.180) | data formatting | bytes 2097152 | tf_op jit(solution)/shard_map/reshape.20
  63.9 2.0 convert_bitcast_fusion
  65.8 1.2 copy.33
  67.0 2.8 fusion.4
  69.8 0.0 all-reduce.3.cloned.1.call-update
  69.8 0.0 all-reduce.5.cloned.1.call-start
  69.9 2.1 copy.22
  72.0 78.6 %all-reduce.3.cloned.1.call-done = f32[1,512,512]{1,2,0:T(8,128)} async-done(((f32[1,512,512]{1,2,0:T(8,128)}), f32[1,512,512]{1,2,0:T(8,128)}) %all-reduce.3.cloned.1.call-update) | async-done | bytes 1048592 | tf_op jit(solution)/shard_map/psum | solution.py:120
  150.5 1.7 multiply_subtract_fusion
  152.3 0.3 copy-done.2
  152.6 0.7 fusion.36
  153.4 5.0 %fusion.21 = bf16[1,2,512,8,64]{2,3,4,1,0:T(8,128)(2,1)} fusion(f32[2,512,8,2,64]{1,4,3,0,2:T(8,128)S(1)} %bitcast.178, s32[8,2]{0,1:T(2,128)S(1)} %iota_add_fusion), kind=kOutput, calls=%fused_computation.30 | convolution fusion | flops 101187712 | bytes 5242944 | tf_op jit(solution)/shard_map/pcxktb,ktn->pcxnb/dot_general | solution.py:79
  158.4 4.1 %copy.36 = bf16[1,2,512,8,64]{4,3,2,1,0:T(8,128)(2,1)} copy(bf16[1,2,512,8,64]{2,3,4,1,0:T(8,128)(2,1)} %fusion.21) | data formatting | bytes 2097152 | tf_op jit(solution)/shard_map/convert_element_type | solution.py:81
  162.5 4.0 %reshape.402 = bf16[2,8,64,512]{3,2,1,0:T(8,128)(2,1)} reshape(bf16[1,2,512,8,64]{4,3,2,1,0:T(8,128)(2,1)} %copy.36) | data formatting | bytes 2097152 | tf_op jit(solution)/shard_map/reshape.31
  166.6 2.0 fusion.41
  168.5 3.9 %fusion.24 = bf16[1,2,8,64,512]{4,2,3,1,0:T(8,128)(2,1)S(1)} fusion(f32[2,8,2,64,512]{4,3,2,0,1:T(8,128)S(1)} %bitcast.179, s32[8,2]{0,1:T(2,128)S(1)} %iota_add_fusion), kind=kOutput, calls=%fused_computation.31 | convolution fusion | flops 101187712 | bytes 5242944 | tf_op jit(solution)/shard_map/pcktbx,ktn->pcnbx/dot_general | solution.py:85
  172.4 0.0 copy-start.10
  172.4 0.0 copy-start.11
  172.4 0.3 copy.39
  172.7 0.9 copy-done.10
  173.6 0.3 copy-done.11
  173.9 1.3 fusion.27
  175.3 1.3 convolution_bitcast_fusion
  176.6 0.0 copy-done.1
  176.6 2.1 add_bitcast_fusion
  178.7 1.6 maximum_bitcast_fusion
  180.2 0.0 all-reduce.5.cloned.1.call-update
  180.3 0.0 reduce-scatter.2.cloned.1.call-start
  180.3 1.1 copy-done.3
  181.5 0.3 copy-done.4
  181.8 1.6 maximum_multiply_fusion
  183.3 1.9 copy.41
  185.3 2.4 broadcast_in_dim.2
  187.7 11.6 %dynamic_update_slice.3 = f32[2,768,768]{2,1,0:T(8,128)} dynamic-update-slice(f32[2,768,768]{2,1,0:T(8,128)} %broadcast_in_dim.2, f32[2,512,512]{2,1,0:T(8,128)S(1)} %copy.41, s32[]{:T(128)} %constant.29.clone.1, s32[]{:T(128)S(6)} %select_n.55, s32[]{:T(128)S(6)} %select_n.56) | dynamic-update-slice | bytes 4194308 | tf_op jit(solution)/shard_map/dynamic_update_slice | solution.py:139
  199.2 0.0 reduce-scatter.2.cloned.1.call-update
  199.3 2.0 all-reduce.5.cloned.1.call-done
  201.2 2.9 copy.42
  204.1 78.3 %reduce-scatter.2.cloned.1.call-done = f32[2,48,768]{2,1,0:T(8,128)} async-done(((f32[2,768,768]{2,1,0:T(8,128)}), f32[2,48,768]{2,1,0:T(8,128)}) %reduce-scatter.2.cloned.1.call-update) | async-done | bytes 294928 | tf_op jit(solution)/shard_map/reduce_scatter | solution.py:140
  (11 shorter events, 0.0 us)
Async XLA Ops:
  7.2 47.1 %copy-start = (bf16[1,8,64,128]{3,2,1,0:T(8,128)(2,1)S(1)}, bf16[1,8,64,128]{3,2,1,0:T(8,128)(2,1)}, u32[]{:S(2)}) copy-start(bf16[1,8,64,128]{3,2,1,0:T(8,128)(2,1)} %param.8) | copy-start | bytes 393220
  7.2 18.7 %copy-start.12 = (s32[1,8]{1,0:T(1,128)S(1)}, s32[1,8]{1,0:T(1,128)}, u32[]{:S(2)}) copy-start(s32[1,8]{1,0:T(1,128)} %param.9) | copy-start | bytes 100
  7.2 143.4 %all-reduce.3.cloned.1.call-start = ((), (), s32[]{:S(2)}) async-start(), calls=%async_computation.1 | async-start | bytes 2097152 | tf_op jit(solution)/shard_map/psum | solution.py:120
  40.0 3.0 %copy-start.5 = (bf16[1,512,512]{2,1,0:T(8,128)(2,1)S(1)}, bf16[1,512,512]{2,1,0:T(8,128)(2,1)}, u32[]{:S(2)}) copy-start(bf16[1,512,512]{2,1,0:T(8,128)(2,1)} %multiply_convert_fusion.2) | copy-start | bytes 1572868
  40.0 3.0 %copy-start.6 = (bf16[1,512,512]{2,1,0:T(8,128)(2,1)S(1)}, bf16[1,512,512]{2,1,0:T(8,128)(2,1)}, u32[]{:S(2)}) copy-start(bf16[1,512,512]{2,1,0:T(8,128)(2,1)} %get-tuple-element.26) | copy-start | bytes 1572868
  40.0 3.0 %copy-start.7 = (bf16[1,512,512]{2,1,0:T(8,128)(2,1)S(1)}, bf16[1,512,512]{2,1,0:T(8,128)(2,1)}, u32[]{:S(2)}) copy-start(bf16[1,512,512]{2,1,0:T(8,128)(2,1)} %get-tuple-element.27) | copy-start | bytes 1572868
  40.0 3.0 %copy-start.8 = (bf16[1,512,512]{2,1,0:T(8,128)(2,1)S(1)}, bf16[1,512,512]{2,1,0:T(8,128)(2,1)}, u32[]{:S(2)}) copy-start(bf16[1,512,512]{2,1,0:T(8,128)(2,1)} %get-tuple-element.24) | copy-start | bytes 1572868
  40.0 3.0 %copy-start.9 = (bf16[1,512,512]{2,1,0:T(8,128)(2,1)S(1)}, bf16[1,512,512]{2,1,0:T(8,128)(2,1)}, u32[]{:S(2)}) copy-start(bf16[1,512,512]{2,1,0:T(8,128)(2,1)} %get-tuple-element.25) | copy-start | bytes 1572868
  69.8 131.4 %all-reduce.5.cloned.1.call-start = ((), (), s32[]{:S(2)}) async-start(), calls=%async_computation.3 | async-start | bytes 4194304 | tf_op jit(solution)/shard_map/psum | solution.py:136
  150.5 2.1 copy-start.2
  172.4 1.2 copy-start.10
  172.4 1.5 copy-start.11
  175.3 1.3 copy-start.1
  180.2 1.2 copy-start.3
  180.2 1.5 copy-start.4
  180.3 102.1 %reduce-scatter.2.cloned.1.call-start = ((), (), s32[]{:S(2)}) async-start(), calls=%async_computation.2 | async-start | bytes 5013504 | tf_op jit(solution)/shard_map/reduce_scatter | solution.py:140
Sparse Core Ops, SparseCore 0:
  70.0 80.5 all-reduce.2
  180.4 20.7 all-reduce.4
  205.7 76.6 reduce-scatter.1
where the time goes:
time: 290 us; the launch traced here: 289 us
  waiting for transfers between devices  159 us (55%)
  local copies, waits for them, and re-layouts  58 us (20%)
  matrix products  27.3 us (9%)
  other arithmetic  26.8 us (9%)
  between operations  17.8 us (6%)
    psum x1, waiting for transfers between devices, local(): intensity_all = lax.psum(intensity_sum, 'wave')  78.6 us
    reduce_scatter x1, waiting for transfers between devices, local(): lax.psum_scatter(object_local, ('wave', 'pos'), scatter_dimension=1, tile...  78.3 us
    another operation x3, other arithmetic  14.7 us
    another operation x3, local copies, waits for them, and re-layouts  12.1 us
    unnamed x30, local copies, waits for them, and re-layouts  12.1 us
    dynamic_update_slice x1, local copies, waits for them, and re-layouts, local(): lax.dynamic_update_slice(object_local, patch_total[0], corners[0])  11.6 us
    dot_general x2, matrix products, complex_right(): jnp.einsum('pcxm,dcmy->pdxy', values, matrix, preferred_element_type=jnp....  7.13 us
  transfers between devices with their start and end apart: 3, of which 3 were waited for; matrix products, arithmetic and copies ran while one was open for 8% of the time, Pallas kernels for 0%

commit v1 on v0

v1 whole, which is shorter than its diff:
```python
import functools
import math

import jax
import jax.numpy as jnp
import numpy as np
from jax import lax
from jax.experimental import pallas as pl
from jax.experimental.pallas import tpu as pltpu
from jax.sharding import PartitionSpec as P

MESH = pl.DeviceIdType.MESH
LANES = 4
VMEM_BYTES = 52 * 1024 * 1024
F32 = jnp.float32
BF16 = jnp.bfloat16


def dft_tables(length):
    line = np.arange(length, dtype=np.int64)
    angles = (line[:, None] * line[None, :] % length) * (2.0 * math.pi / length)
    real = np.cos(angles) / math.sqrt(length)
    imag = -np.sin(angles) / math.sqrt(length)
    right = np.block([[real, imag], [-imag, real]]).astype(np.float32).astype(jnp.bfloat16)
    left = np.block([[real, -imag], [imag, real]]).astype(np.float32).astype(jnp.bfloat16)
    return jnp.asarray(left), jnp.asarray(right)


def bit_count(waves):
    return waves.bit_length() - 1


def bit_order(lane, bits):
    order = list(range(bits))
    if lane % 2 and bits > 1:
        order[0], order[1] = 1, 0
    return order


def slot_of(chunk, lane, bits):
    slot = 0
    for bit in bit_order(lane, bits):
        slot = slot * 2 + (chunk >> bit) % 2
    return slot


def dot(a, b, contract=((1,), (0,))):
    return lax.dot_general(a, b, (contract, ((), ())), preferred_element_type=F32)


def forward_kernel(
    waves, off_ref, band_ref, obj_ref, probe_ref, blk_ref, left_ref, right_ref,
    patch_ref, det_ref, map_ref, inten_ref, exit_s, half_s, far_s, rows_s,
):
    side = probe_ref.shape[1]
    obj_side = obj_ref.shape[2]
    bits = bit_count(waves)
    tile = 64
    row0 = off_ref[0, 0]
    base = jnp.minimum(row0 // 8 * 8, obj_side - side - 8)
    lift = tile + 8 - (row0 - base)
    shift = lax.rem(obj_side - off_ref[1, 0], obj_side)
    for t in range(side // tile):
        rows = pl.ds(t * tile, tile)
        parts = []
        for c in range(2):
            wide = obj_ref[c, pl.ds(pl.multiple_of(base + t * tile, 8), tile + 8), :]
            part = pltpu.roll(wide, shift, axis=1)[:, :side]
            part = pltpu.roll(part, lax.rem(lift, tile + 8), axis=0)[:tile]
            patch_ref[c, rows, :] = part
            parts.append(part)
        pr, pi = probe_ref[0, rows, :], probe_ref[1, rows, :]
        exit_s[rows, :] = (pr * parts[0] - pi * parts[1]).astype(BF16)
        exit_s[pl.ds(side + t * tile, tile), :] = (pr * parts[1] + pi * parts[0]).astype(BF16)
    blocks, brows, bwidth = blk_ref.shape
    lane_block = lax.broadcasted_iota(jnp.int32, (brows, side), 1) // brows
    for k in range(blocks):
        start = band_ref[0, k]
        blk = blk_ref[k].astype(F32)
        swapped = jnp.concatenate([blk[:, brows:], blk[:, :brows]], axis=1)
        odd = (start % 2).astype(F32)
        chosen = jnp.where(odd > 0.5, swapped, blk)
        wide = jnp.concatenate([chosen] * (side // bwidth), axis=1)
        inside = (lane_block >= start) & (lane_block < start + bwidth // brows)
        map_ref[pl.ds(k * brows, brows), :] = jnp.where(inside, wide, 0.0).astype(BF16)
    step = 256
    per = side // step
    for t in range(2 * per):
        out = dot(left_ref[pl.ds(t * step, step), :], exit_s[...])
        half_s[pl.ds((t % per) * step, step), pl.ds((t // per) * side, side)] = out.astype(BF16)
    for t in range(per):
        rows = pl.ds(t * step, step)
        far_s[rows, :] = dot(half_s[rows, :], right_ref[...]).astype(BF16)
    for t in range(per):
        out = dot(map_ref[pl.ds(t * step, step), :], far_s[...]).astype(BF16)
        rows_s[pl.ds(t * step, step), :] = out[:, :side]
        rows_s[pl.ds(side + t * step, step), :] = out[:, side:]
    height = side // waves
    width = side // LANES
    for t in range(per):
        total = None
        for c in range(2):
            rows = pl.ds(c * side + t * step, step)
            out = dot(rows_s[rows, :], map_ref[...], ((1,), (1,)))
            det_ref[rows, :] = out
            total = out * out if total is None else total + out * out
        for j in range(step // height):
            chunk = t * (step // height) + j
            for lane in range(LANES):
                inten_ref[lane, slot_of(chunk, lane, bits)] = total[
                    j * height : (j + 1) * height, lane * width : (lane + 1) * width
                ]


class Halving:
    def __init__(self, waves, buf, land, send, recv):
        self.bits = bit_count(waves)
        self.waves, self.buf, self.land, self.send, self.recv = waves, buf, land, send, recv
        self.me = lax.axis_index("wave")

    def bit(self, lane, step):
        return (self.me // 2 ** bit_order(lane, self.bits)[step]) % 2

    def partner(self, lane, step):
        return self.me + (1 - 2 * self.bit(lane, step)) * 2 ** bit_order(lane, self.bits)[step]

    def base(self, lane, step):
        return sum((self.bit(lane, s) * (self.waves >> (s + 1)) for s in range(step)), 0)

    def down(self, lane, step):
        half = self.waves >> (step + 1)
        first = self.base(lane, step) + (1 - self.bit(lane, step)) * half
        return pltpu.make_async_remote_copy(
            src_ref=self.buf.at[lane, pl.ds(first, half)],
            dst_ref=self.land.at[lane, pl.ds(half, half)],
            send_sem=self.send.at[lane, step],
            recv_sem=self.recv.at[lane, step],
            device_id={"wave": self.partner(lane, step)},
            device_id_type=MESH,
        )

    def add(self, lane, step):
        half = self.waves >> (step + 1)
        first = self.base(lane, step + 1)
        for k in range(half):
            self.buf[lane, first + k] = self.buf[lane, first + k] + self.land[lane, half + k]

    def up(self, full, lane, step):
        half = self.waves >> (step + 1)
        mine = pl.ds(self.base(lane, step + 1), half)
        return pltpu.make_async_remote_copy(
            src_ref=full.at[lane, mine],
            dst_ref=full.at[lane, mine],
            send_sem=self.send.at[lane, self.bits + step],
            recv_sem=self.recv.at[lane, self.bits + step],
            device_id={"wave": self.partner(lane, step)},
            device_id_type=MESH,
        )


def greet(waves, cores):
    bits = bit_count(waves)
    me = lax.axis_index("wave")
    barrier = pltpu.get_barrier_semaphore()
    for b in range(bits):
        other = me + (1 - 2 * ((me // 2**b) % 2)) * 2**b
        pl.semaphore_signal(barrier, inc=1, device_id={"wave": other}, device_id_type=MESH)
    if cores:
        pl.semaphore_signal(
            barrier, inc=1, device_id={"pos": 1 - lax.axis_index("pos")}, device_id_type=MESH
        )
    pl.semaphore_wait(barrier, bits + int(cores))


def sum_kernel(waves, in_ref, out_ref, buf, land, full, send, recv):
    bits = bit_count(waves)
    ring = Halving(waves, buf, land, send, recv)
    greet(waves, False)
    buf[...] = in_ref[...]
    copies = []
    flying = {}
    for step in range(bits):
        for lane in range(LANES):
            if step:
                flying[lane].wait_recv()
                ring.add(lane, step - 1)
            copy = ring.down(lane, step)
            copy.start()
            flying[lane] = copy
            copies.append(copy)
    for step in reversed(range(bits)):
        for lane in range(LANES):
            flying[lane].wait_recv()
            if step == bits - 1:
                spot = ring.base(lane, bits)
                full[lane, spot] = buf[lane, spot] + land[lane, 1]
            copy = ring.up(full, lane, step)
            copy.start()
            flying[lane] = copy
            copies.append(copy)
    for lane in range(LANES):
        flying[lane].wait_recv()
    for copy in copies:
        copy.wait_send()
    out_ref[...] = full[...]


def backward_kernel(
    waves, off_ref, det_ref, total_ref, meas_ref, map_ref, patch_ref, probe_ref, left_ref, right_ref,
    term_ref, place_ref, grad_s, row_s, far_s, half_s, pad_s,
):
    side = probe_ref.shape[1]
    obj_side = pad_s.shape[2]
    margin = obj_side - side
    bits = bit_count(waves)
    height = side // waves
    width = side // LANES
    for chunk in range(waves):
        rows = pl.ds(chunk * height, height)
        total = jnp.concatenate(
            [total_ref[lane, slot_of(chunk, lane, bits)] for lane in range(LANES)], axis=1
        )
        factor = 1.0 - meas_ref[rows, :].astype(F32) / jnp.sqrt(total * (1.0 / waves) + 1.0)
        for c in range(2):
            there = pl.ds(c * side + chunk * height, height)
            grad_s[there, :] = (factor * det_ref[there, :]).astype(BF16)
    for c in range(2):
        pad_s[c, pl.ds(0, margin), :] = jnp.zeros((margin, obj_side), F32)
        pad_s[c, pl.ds(margin + side, margin + 16), :] = jnp.zeros((margin + 16, obj_side), F32)
    step = 256
    per = side // step
    for t in range(2 * per):
        out = dot(grad_s[pl.ds(t * step, step), :], map_ref[...])
        row_s[pl.ds((t % per) * step, step), pl.ds((t // per) * side, side)] = out.astype(BF16)
    for t in range(per):
        rows = pl.ds(t * step, step)
        far_s[rows, :] = dot(map_ref[:, t * step : (t + 1) * step], row_s[...], ((0,), (0,))).astype(BF16)
    for t in range(per):
        rows = pl.ds(t * step, step)
        out = dot(far_s[rows, :], left_ref[...]).astype(BF16)
        half_s[rows, :] = out[:, :side]
        half_s[pl.ds(side + t * step, step), :] = out[:, side:]
    shift = off_ref[1, 0]
    scale = 1.0 / waves
    fill = jnp.zeros((step, margin), F32)
    for t in range(per):
        rows = pl.ds(t * step, step)
        er = dot(right_ref[rows, :], half_s[...])
        ei = dot(right_ref[pl.ds(side + t * step, step), :], half_s[...])
        ar, ai = patch_ref[0, rows, :], patch_ref[1, rows, :]
        term_ref[0, rows, :] = ar * er + ai * ei
        term_ref[1, rows, :] = ar * ei - ai * er
        pr, pi = probe_ref[0, rows, :], probe_ref[1, rows, :]
        real = (pr * er + pi * ei) * scale
        imag = (pr * ei - pi * er) * scale
        pad_s[0, pl.ds(margin + t * step, step), :] = pltpu.roll(
            jnp.concatenate([real, fill], axis=1), shift, axis=1
        )
        pad_s[1, pl.ds(margin + t * step, step), :] = pltpu.roll(
            jnp.concatenate([imag, fill], axis=1), shift, axis=1
        )
    tall = place_ref.shape[3]
    wide = place_ref.shape[4]
    first = margin - off_ref[0, 0]
    for c in range(2):
        for owner in range(2 * waves):
            start = first + owner * tall
            tiles = (tall + 7) // 8 * 8 + 8
            block = pad_s[c, pl.ds(pl.multiple_of(start // 8 * 8, 8), tiles), :]
            block = pltpu.roll(block, lax.rem(tiles - start % 8, tiles), axis=0)[:tall]
            for part in range(LANES // 2):
                lane = 2 * part + c
                place_ref[owner % 2, lane, slot_of(owner // 2, lane, bits)] = block[
                    :, part * wide : (part + 1) * wide
                ]


def scatter_kernel(
    waves, place_ref, term_ref, obj_ref, probe_ref, buf, land, cross, other, send, recv, csend, crecv
):
    bits = bit_count(waves)
    ring = Halving(waves, buf, land, send, recv)
    mine = lax.axis_index("pos")
    greet(waves, True)

    def to_core(source, target, index):
        return pltpu.make_async_remote_copy(
            src_ref=source, dst_ref=target, send_sem=csend.at[index], recv_sem=crecv.at[index],
            device_id={"pos": 1 - mine}, device_id_type=MESH,
        )

    swaps = [to_core(place_ref.at[1 - mine, lane], cross.at[lane], lane) for lane in range(LANES)]
    terms = [to_core(term_ref.at[c], other.at[c], LANES + c) for c in range(2)]
    for copy in swaps + terms:
        copy.start()
    copies = swaps + terms
    flying = {}
    for step in range(bits):
        for lane in range(LANES):
            if step:
                flying[lane].wait_recv()
                ring.add(lane, step - 1)
            else:
                swaps[lane].wait_recv()
                for k in range(waves):
                    buf[lane, k] = place_ref[mine, lane, k] + cross[lane, k]
            copy = ring.down(lane, step)
            copy.start()
            flying[lane] = copy
            copies.append(copy)
    for c in range(2):
        terms[c].wait_recv()
        probe_ref[c] = term_ref[c] + other[c]
    wide = buf.shape[3]
    for lane in range(LANES):
        flying[lane].wait_recv()
        spot = ring.base(lane, bits)
        obj_ref[lane % 2, :, pl.ds((lane // 2) * wide, wide)] = buf[lane, spot] + land[lane, 1]
    for copy in copies:
        copy.wait_send()


def local(waves, object_field, probe_field, resample_blocks, band_start, measured, offsets):
    side = probe_field.shape[2]
    obj_side = object_field.shape[1]
    bits = bit_count(waves)
    left, right = dft_tables(side)
    probe = probe_field[0]
    vmem = pl.BlockSpec(memory_space=pltpu.VMEM)
    smem = pl.BlockSpec(memory_space=pltpu.SMEM)
    shape = jax.ShapeDtypeStruct
    plain = pltpu.CompilerParams(vmem_limit_bytes=VMEM_BYTES)
    lanes_shape = (LANES, waves, side // waves, side // LANES)
    patch, det, dense, inten = pl.pallas_call(
        functools.partial(forward_kernel, waves),
        out_shape=(
            shape((2, side, side), F32), shape((2 * side, side), F32), shape((side, side), BF16),
            shape(lanes_shape, F32),
        ),
        in_specs=[smem, smem] + [vmem] * 5,
        out_specs=(vmem,) * 4,
        scratch_shapes=[
            pltpu.VMEM((2 * side, side), BF16), pltpu.VMEM((side, 2 * side), BF16),
            pltpu.VMEM((side, 2 * side), BF16), pltpu.VMEM((2 * side, side), BF16),
        ],
        compiler_params=plain,
        name="forward",
    )(offsets, band_start, object_field, probe, resample_blocks[0], left, right)
    total = pl.pallas_call(
        functools.partial(sum_kernel, waves),
        out_shape=shape(lanes_shape, F32),
        in_specs=[vmem],
        out_specs=vmem,
        scratch_shapes=[
            pltpu.VMEM(lanes_shape, F32), pltpu.VMEM(lanes_shape, F32), pltpu.VMEM(lanes_shape, F32),
            pltpu.SemaphoreType.DMA((LANES, 2 * bits)), pltpu.SemaphoreType.DMA((LANES, 2 * bits)),
        ],
        compiler_params=pltpu.CompilerParams(
            vmem_limit_bytes=VMEM_BYTES, collective_id=0, has_side_effects=True
        ),
        name="intensity_sum",
    )(inten)
    tall = obj_side // (2 * waves)
    wide = 2 * obj_side // LANES
    place_shape = (LANES, waves, tall, wide)
    term, place = pl.pallas_call(
        functools.partial(backward_kernel, waves),
        out_shape=(shape((2, side, side), F32), shape((2,) + place_shape, F32)),
        in_specs=[smem] + [vmem] * 8,
        out_specs=(vmem,) * 2,
        scratch_shapes=[
            pltpu.VMEM((2 * side, side), BF16), pltpu.VMEM((side, 2 * side), BF16),
            pltpu.VMEM((side, 2 * side), BF16), pltpu.VMEM((2 * side, side), BF16),
            pltpu.VMEM((2, 2 * obj_side - side + 16, obj_side), F32),
        ],
        compiler_params=plain,
        name="backward",
    )(offsets, det, total, measured[0], dense, patch, probe, left, right)
    object_grad, probe_grad = pl.pallas_call(
        functools.partial(scatter_kernel, waves),
        out_shape=(shape((2, tall, obj_side), F32), shape((2, side, side), F32)),
        in_specs=[vmem] * 2,
        out_specs=(vmem,) * 2,
        scratch_shapes=[
            pltpu.VMEM(place_shape, F32), pltpu.VMEM(place_shape, F32), pltpu.VMEM(place_shape, F32),
            pltpu.VMEM((2, side, side), F32),
            pltpu.SemaphoreType.DMA((LANES, bits)), pltpu.SemaphoreType.DMA((LANES, bits)),
            pltpu.SemaphoreType.DMA((LANES + 2,)), pltpu.SemaphoreType.DMA((LANES + 2,)),
        ],
        compiler_params=pltpu.CompilerParams(
            vmem_limit_bytes=VMEM_BYTES, collective_id=1, has_side_effects=True
        ),
        name="object_sum",
    )(place, term)
    return object_grad, probe_grad[None]


def solution(mesh):
    in_specs = (
        P(None, "parts", None),
        P("wave", None, "parts", None),
        P("wave", None, None, None),
        P("wave", None),
        P("pos", "parts", None),
        P("parts", "pos"),
    )
    out_specs = (P(None, ("parts", "wave", "pos"), None), P("wave", None, "parts", None))
    step = functools.partial(local, mesh.shape["wave"])
    return jax.shard_map(step, mesh=mesh, in_specs=in_specs, out_specs=out_specs, check_vma=False)
```

time: 290 us -> 110 us (0.38)
  waiting for transfers between devices: 159 us -> 0 us
  Pallas kernels: 0 us -> 101 us
  local copies, waits for them, and re-layouts: 58 us -> 8.05 us
  matrix products: 27.3 us -> 0 us
  other arithmetic: 26.8 us -> 0 us
  between operations: 17.8 us -> 0.66 us
    pallas_call x0 -> x4, Pallas kernels: none -> 101 us  [the longest x1 41 us: local(): pl.pallas_call(functools.partial(scatter_kernel, waves), out_shape=(shape...]
    psum x2 -> x0, waiting for transfers between devices: 80.5 us -> none  [the longest x1 78.6 us: local(): intensity_all = lax.psum(intensity_sum, 'wave')]
    reduce_scatter x1 -> x0, waiting for transfers between devices: 78.3 us -> none  [local(): lax.psum_scatter(object_local, ('wave', 'pos'), scatter_dimension=1, tile...]
    dot_general x11 -> x0, matrix products: 27.3 us -> none  [the longest x2 7.13 us: complex_right(): jnp.einsum('pcxm,dcmy->pdxy', values, matrix, preferred_element_type=jnp....]
    another operation x6 -> x0, other arithmetic: 21.4 us -> none
    another operation x3 -> x0, local copies, waits for them, and re-layouts: 12.1 us -> none
    dynamic_update_slice x1 -> x0, local copies, waits for them, and re-layouts: 11.6 us -> none  [local(): lax.dynamic_update_slice(object_local, patch_total[0], corners[0])]
    convert_element_type x5 -> x0, local copies, waits for them, and re-layouts: 7.87 us -> none  [the longest x1 4.15 us: backward_pass(): row_grad = jnp.einsum('pcxktb,ktn->pcxnb', spread, picker, precision=lax....]
  transfers between devices with their start and end apart: 3 -> 0, of which waited for: 3 -> 0; matrix products, arithmetic and copies ran while one was open for 8% -> 0% of each run, Pallas kernels for 0% -> 0%
where the time goes in v1:
time: 110 us
  Pallas kernels  101 us (92%)
  local copies, waits for them, and re-layouts  8.05 us (7%)
    pallas_call x1, Pallas kernels, local(): pl.pallas_call(functools.partial(scatter_kernel, waves), out_shape=(shape...  41 us
    pallas_call x1, Pallas kernels, local(): pl.pallas_call(functools.partial(sum_kernel, waves), out_shape=shape(lane...  36.1 us
    pallas_call x1, Pallas kernels, local(): pl.pallas_call(functools.partial(backward_kernel, waves), out_shape=(shap...  12.8 us
    pallas_call x1, Pallas kernels, local(): pl.pallas_call(functools.partial(forward_kernel, waves), out_shape=(shape...  10.9 us
    unnamed x13, local copies, waits for them, and re-layouts  8.05 us

profile of v1, /device:TPU:0, one launch (start us, length us, event | category | flops | bytes accessed | tf_op | source)
XLA Modules:
  0.0 109.6 jit_solution(69660846663601733)
XLA Ops:
  0.6 0.7 copy.11.off_ref
  1.4 0.0 copy-start.3
  1.4 0.9 copy-done.3
  2.3 0.0 copy-start.4
  2.3 0.7 copy-done.4
  2.9 10.9 %forward.1 = (f32[2,512,512]{2,1,0:T(8,128)}, f32[1024,512]{1,0:T(8,128)}, bf16[512,512]{1,0:T(8,128)(2,1)S(1)}, f32[4,8,64,128]{3,2,1,0:T(8,128)S(1)}) custom-call(s32[2,1]{1,0:T(2,128)S(1)} %copy.11.off_ref, s32[1,8]{1,0:T(1,128)S(1)} %copy-done.4, f32[2,768,768]{2,1,0:T(8,128)} %obj_ref.1, f32[2,512,512]{2,1,0:T(8,128)} %bitcast.6, ...), custom_call_target="tpu_custom_call" | custom-call | tf_op jit(solution)/shard_map/forward/pallas_call | solution.py:334
  13.8 0.0 copy-start.1
  13.8 1.0 copy-done.1
  14.8 0.0 copy-start.2
  14.8 36.1 %intensity_sum.1.total_ref = f32[4,8,64,128]{3,2,1,0:T(8,128)S(1)} custom-call(f32[4,8,64,128]{3,2,1,0:T(8,128)} %copy-done.1), custom_call_target="tpu_custom_call" | custom-call | tf_op jit(solution)/shard_map/intensity_sum/pallas_call | solution.py:349
  50.9 0.0 copy-start
  50.9 1.0 copy-done
  51.9 0.0 copy-done.2
  51.9 12.8 %backward.1 = (f32[2,512,512]{2,1,0:T(8,128)}, f32[2,4,8,48,384]{4,3,2,1,0:T(8,128)}) custom-call(s32[2,1]{1,0:T(2,128)S(1)} %copy.11.off_ref, f32[1024,512]{1,0:T(8,128)} %get-tuple-element.10.det_ref, f32[4,8,64,128]{3,2,1,0:T(8,128)} %copy-done, bf16[512,512]{1,0:T(8,128)(2,1)S(1)} %bitcast.4, bf16[512,512]{1,0:T(8,128)(2,1)S(1)} %get-tuple-element.12.map_ref, ...), custom_call_target="tpu_custom_call" | custom-call | tf_op jit(solution)/shard_map/backward/pallas_call | solution.py:366
  64.8 41.0 %object_sum.1 = (f32[2,48,768]{2,1,0:T(8,128)S(1)}, f32[2,512,512]{2,1,0:T(8,128)}) custom-call(f32[2,4,8,48,384]{4,3,2,1,0:T(8,128)} %get-tuple-element.14.place_ref, f32[2,512,512]{2,1,0:T(8,128)} %get-tuple-element.15.term_ref), custom_call_target="tpu_custom_call" | custom-call | tf_op jit(solution)/shard_map/object_sum/pallas_call | solution.py:379
  105.8 0.7 copy.14
  106.5 3.1 %copy.15 = f32[1,2,512,512]{3,2,1,0:T(8,128)} copy(f32[1,2,512,512]{3,2,1,0:T(8,128)} %bitcast.8) | data formatting | bytes 4194304
Async XLA Ops:
  1.4 0.9 copy-start.3
  2.3 0.7 copy-start.4
  13.8 1.0 copy-start.1
  14.8 37.1 %copy-start.2 = (bf16[1,512,512]{2,1,0:T(8,128)(2,1)S(1)}, bf16[1,512,512]{2,1,0:T(8,128)(2,1)}, u32[]{:S(2)}) copy-start(bf16[1,512,512]{2,1,0:T(8,128)(2,1)} %param.12) | copy-start | bytes 1572868
  50.9 1.0 copy-start

commit v2 on v1

--- a/solution.py
+++ b/solution.py
@@ -10,7 +10,9 @@
 from jax.sharding import PartitionSpec as P
 
 MESH = pl.DeviceIdType.MESH
-LANES = 4
+SUM_LANES = 8
+GROUP = 100
+MIX = 2
 VMEM_BYTES = 52 * 1024 * 1024
 F32 = jnp.float32
 BF16 = jnp.bfloat16
@@ -32,7 +34,7 @@
 
 def bit_order(lane, bits):
     order = list(range(bits))
-    if lane % 2 and bits > 1:
+    if lane % MIX == MIX - 1 and bits > 1:
         order[0], order[1] = 1, 0
     return order
 
@@ -96,7 +98,7 @@
         rows_s[pl.ds(t * step, step), :] = out[:, :side]
         rows_s[pl.ds(side + t * step, step), :] = out[:, side:]
     height = side // waves
-    width = side // LANES
+    width = side // (SUM_LANES // 2)
     for t in range(per):
         total = None
         for c in range(2):
@@ -106,10 +108,21 @@
             total = out * out if total is None else total + out * out
         for j in range(step // height):
             chunk = t * (step // height) + j
-            for lane in range(LANES):
+            for lane in range(SUM_LANES):
+                top = j * height + lane % 2 * (height // 2)
+                first = lane // 2 * width
                 inten_ref[lane, slot_of(chunk, lane, bits)] = total[
-                    j * height : (j + 1) * height, lane * width : (lane + 1) * width
+                    top : top + height // 2, first : first + width
                 ]
+
+
+def diagonal(lanes, steps):
+    def key(item):
+        lane, step = item
+        group = lane // GROUP
+        return (group - 1 if step == 0 else group + step, step, lane)
+
+    return sorted([(lane, step) for lane in range(lanes) for step in range(steps)], key=key)
 
 
 class Halving:
@@ -179,26 +192,22 @@
     buf[...] = in_ref[...]
     copies = []
     flying = {}
-    for step in range(bits):
-        for lane in range(LANES):
+    for lane, step in diagonal(SUM_LANES, 2 * bits):
+        if step:
+            flying[lane].wait_recv()
+        if step < bits:
             if step:
-                flying[lane].wait_recv()
                 ring.add(lane, step - 1)
             copy = ring.down(lane, step)
-            copy.start()
-            flying[lane] = copy
-            copies.append(copy)
-    for step in reversed(range(bits)):
-        for lane in range(LANES):
-            flying[lane].wait_recv()
-            if step == bits - 1:
+        else:
+            if step == bits:
                 spot = ring.base(lane, bits)
                 full[lane, spot] = buf[lane, spot] + land[lane, 1]
-            copy = ring.up(full, lane, step)
-            copy.start()
-            flying[lane] = copy
-            copies.append(copy)
-    for lane in range(LANES):
+            copy = ring.up(full, lane, 2 * bits - 1 - step)
+        copy.start()
+        flying[lane] = copy
+        copies.append(copy)
+    for lane in range(SUM_LANES):
         flying[lane].wait_recv()
     for copy in copies:
         copy.wait_send()
@@ -214,15 +223,16 @@
     margin = obj_side - side
     bits = bit_count(waves)
     height = side // waves
-    width = side // LANES
-    for chunk in range(waves):
-        rows = pl.ds(chunk * height, height)
+    for piece in range(2 * waves):
+        chunk, half = piece // 2, piece % 2
+        rows = pl.ds(piece * (height // 2), height // 2)
         total = jnp.concatenate(
-            [total_ref[lane, slot_of(chunk, lane, bits)] for lane in range(LANES)], axis=1
+            [total_ref[lane, slot_of(chunk, lane, bits)] for lane in range(half, SUM_LANES, 2)],
+            axis=1,
         )
         factor = 1.0 - meas_ref[rows, :].astype(F32) / jnp.sqrt(total * (1.0 / waves) + 1.0)
         for c in range(2):
-            there = pl.ds(c * side + chunk * height, height)
+            there = pl.ds(c * side + piece * (height // 2), height // 2)
             grad_s[there, :] = (factor * det_ref[there, :]).astype(BF16)
     for c in range(2):
         pad_s[c, pl.ds(0, margin), :] = jnp.zeros((margin, obj_side), F32)
@@ -268,7 +278,7 @@
             tiles = (tall + 7) // 8 * 8 + 8
             block = pad_s[c, pl.ds(pl.multiple_of(start // 8 * 8, 8), tiles), :]
             block = pltpu.roll(block, lax.rem(tiles - start % 8, tiles), axis=0)[:tall]
-            for part in range(LANES // 2):
+            for part in range(place_ref.shape[1] // 2):
                 lane = 2 * part + c
                 place_ref[owner % 2, lane, slot_of(owner // 2, lane, bits)] = block[
                     :, part * wide : (part + 1) * wide
@@ -289,30 +299,30 @@
             device_id={"pos": 1 - mine}, device_id_type=MESH,
         )
 
-    swaps = [to_core(place_ref.at[1 - mine, lane], cross.at[lane], lane) for lane in range(LANES)]
-    terms = [to_core(term_ref.at[c], other.at[c], LANES + c) for c in range(2)]
-    for copy in swaps + terms:
+    lanes = place_ref.shape[1]
+    swaps = [to_core(place_ref.at[1 - mine, lane], cross.at[lane], lane) for lane in range(lanes)]
+    terms = [to_core(term_ref.at[c], other.at[c], lanes + c) for c in range(2)]
+    copies = swaps + terms
+    for copy in copies:
         copy.start()
-    copies = swaps + terms
     flying = {}
-    for step in range(bits):
-        for lane in range(LANES):
-            if step:
-                flying[lane].wait_recv()
-                ring.add(lane, step - 1)
-            else:
-                swaps[lane].wait_recv()
-                for k in range(waves):
-                    buf[lane, k] = place_ref[mine, lane, k] + cross[lane, k]
-            copy = ring.down(lane, step)
-            copy.start()
-            flying[lane] = copy
-            copies.append(copy)
+    for lane, step in diagonal(lanes, bits):
+        if step:
+            flying[lane].wait_recv()
+            ring.add(lane, step - 1)
+        else:
+            swaps[lane].wait_recv()
+            for k in range(waves):
+                buf[lane, k] = place_ref[mine, lane, k] + cross[lane, k]
+        copy = ring.down(lane, step)
+        copy.start()
+        flying[lane] = copy
+        copies.append(copy)
     for c in range(2):
         terms[c].wait_recv()
         probe_ref[c] = term_ref[c] + other[c]
     wide = buf.shape[3]
-    for lane in range(LANES):
+    for lane in range(lanes):
         flying[lane].wait_recv()
         spot = ring.base(lane, bits)
         obj_ref[lane % 2, :, pl.ds((lane // 2) * wide, wide)] = buf[lane, spot] + land[lane, 1]
@@ -330,7 +340,7 @@
     smem = pl.BlockSpec(memory_space=pltpu.SMEM)
     shape = jax.ShapeDtypeStruct
     plain = pltpu.CompilerParams(vmem_limit_bytes=VMEM_BYTES)
-    lanes_shape = (LANES, waves, side // waves, side // LANES)
+    lanes_shape = (SUM_LANES, waves, side // waves // 2, side // (SUM_LANES // 2))
     patch, det, dense, inten = pl.pallas_call(
         functools.partial(forward_kernel, waves),
         out_shape=(
@@ -353,7 +363,8 @@
         out_specs=vmem,
         scratch_shapes=[
             pltpu.VMEM(lanes_shape, F32), pltpu.VMEM(lanes_shape, F32), pltpu.VMEM(lanes_shape, F32),
-            pltpu.SemaphoreType.DMA((LANES, 2 * bits)), pltpu.SemaphoreType.DMA((LANES, 2 * bits)),
+            pltpu.SemaphoreType.DMA((SUM_LANES, 2 * bits)),
+            pltpu.SemaphoreType.DMA((SUM_LANES, 2 * bits)),
         ],
         compiler_params=pltpu.CompilerParams(
             vmem_limit_bytes=VMEM_BYTES, collective_id=0, has_side_effects=True
@@ -361,8 +372,9 @@
         name="intensity_sum",
     )(inten)
     tall = obj_side // (2 * waves)
-    wide = 2 * obj_side // LANES
-    place_shape = (LANES, waves, tall, wide)
+    wide = 128
+    lanes = 2 * obj_side // wide
+    place_shape = (lanes, waves, tall, wide)
     term, place = pl.pallas_call(
         functools.partial(backward_kernel, waves),
         out_shape=(shape((2, side, side), F32), shape((2,) + place_shape, F32)),
@@ -384,8 +396,8 @@
         scratch_shapes=[
             pltpu.VMEM(place_shape, F32), pltpu.VMEM(place_shape, F32), pltpu.VMEM(place_shape, F32),
             pltpu.VMEM((2, side, side), F32),
-            pltpu.SemaphoreType.DMA((LANES, bits)), pltpu.SemaphoreType.DMA((LANES, bits)),
-            pltpu.SemaphoreType.DMA((LANES + 2,)), pltpu.SemaphoreType.DMA((LANES + 2,)),
+            pltpu.SemaphoreType.DMA((lanes, bits)), pltpu.SemaphoreType.DMA((lanes, bits)),
+            pltpu.SemaphoreType.DMA((lanes + 2,)), pltpu.SemaphoreType.DMA((lanes + 2,)),
         ],
         compiler_params=pltpu.CompilerParams(
             vmem_limit_bytes=VMEM_BYTES, collective_id=1, has_side_effects=True

time: 110 us -> 106 us (0.964)
  Pallas kernels: 101 us -> 97 us
    pallas_call x1, Pallas kernels: 41 us -> 38.3 us  [local(): pl.pallas_call(functools.partial(scatter_kernel, waves), out_shape=(shape...]
    pallas_call x1, Pallas kernels: 36.1 us -> 35 us  [local(): pl.pallas_call(functools.partial(sum_kernel, waves), out_shape=shape(lane...]
where the time goes in v2:
time: 106 us
  Pallas kernels  97 us (92%)
  local copies, waits for them, and re-layouts  8.05 us (8%)
    pallas_call x1, Pallas kernels, local(): pl.pallas_call(functools.partial(scatter_kernel, waves), out_shape=(shape...  38.3 us
    pallas_call x1, Pallas kernels, local(): pl.pallas_call(functools.partial(sum_kernel, waves), out_shape=shape(lane...  35 us
    pallas_call x1, Pallas kernels, local(): pl.pallas_call(functools.partial(backward_kernel, waves), out_shape=(shap...  12.8 us
    pallas_call x1, Pallas kernels, local(): pl.pallas_call(functools.partial(forward_kernel, waves), out_shape=(shape...  10.9 us
    unnamed x13, local copies, waits for them, and re-layouts  8.05 us

profile of v2, /device:TPU:0, one launch (start us, length us, event | category | flops | bytes accessed | tf_op | source)
XLA Modules:
  0.0 105.7 jit_solution(11178854144506550559)
XLA Ops:
  0.6 0.7 copy.11.off_ref
  1.4 0.0 copy-start.3
  1.4 0.9 copy-done.3
  2.3 0.0 copy-start.4
  2.3 0.7 copy-done.4
  2.9 10.9 %forward.1 = (f32[2,512,512]{2,1,0:T(8,128)}, f32[1024,512]{1,0:T(8,128)}, bf16[512,512]{1,0:T(8,128)(2,1)S(1)}, f32[8,8,32,128]{3,2,1,0:T(8,128)S(1)}) custom-call(s32[2,1]{1,0:T(2,128)S(1)} %copy.11.off_ref, s32[1,8]{1,0:T(1,128)S(1)} %copy-done.4, f32[2,768,768]{2,1,0:T(8,128)} %obj_ref.1, f32[2,512,512]{2,1,0:T(8,128)} %bitcast.6, ...), custom_call_target="tpu_custom_call" | custom-call | tf_op jit(solution)/shard_map/forward/pallas_call | solution.py:344
  13.8 0.0 copy-start.1
  13.8 1.0 copy-done.1
  14.8 0.0 copy-start.2
  14.8 35.0 %intensity_sum.1.total_ref = f32[8,8,32,128]{3,2,1,0:T(8,128)S(1)} custom-call(f32[8,8,32,128]{3,2,1,0:T(8,128)} %copy-done.1), custom_call_target="tpu_custom_call" | custom-call | tf_op jit(solution)/shard_map/intensity_sum/pallas_call | solution.py:359
  49.8 0.0 copy-start
  49.8 1.0 copy-done
  50.8 0.0 copy-done.2
  50.8 12.8 %backward.1 = (f32[2,512,512]{2,1,0:T(8,128)}, f32[2,12,8,48,128]{4,3,2,1,0:T(8,128)}) custom-call(s32[2,1]{1,0:T(2,128)S(1)} %copy.11.off_ref, f32[1024,512]{1,0:T(8,128)} %get-tuple-element.10.det_ref, f32[8,8,32,128]{3,2,1,0:T(8,128)} %copy-done, bf16[512,512]{1,0:T(8,128)(2,1)S(1)} %bitcast.4, bf16[512,512]{1,0:T(8,128)(2,1)S(1)} %get-tuple-element.12.map_ref, ...), custom_call_target="tpu_custom_call" | custom-call | tf_op jit(solution)/shard_map/backward/pallas_call | solution.py:378
  63.6 38.3 %object_sum.1 = (f32[2,48,768]{2,1,0:T(8,128)S(1)}, f32[2,512,512]{2,1,0:T(8,128)}) custom-call(f32[2,12,8,48,128]{4,3,2,1,0:T(8,128)} %get-tuple-element.14.place_ref, f32[2,512,512]{2,1,0:T(8,128)} %get-tuple-element.15.term_ref), custom_call_target="tpu_custom_call" | custom-call | tf_op jit(solution)/shard_map/object_sum/pallas_call | solution.py:391
  101.9 0.7 copy.14
  102.6 3.1 %copy.15 = f32[1,2,512,512]{3,2,1,0:T(8,128)} copy(f32[1,2,512,512]{3,2,1,0:T(8,128)} %bitcast.8) | data formatting | bytes 4194304
Async XLA Ops:
  1.4 0.9 copy-start.3
  2.3 0.7 copy-start.4
  13.8 1.0 copy-start.1
  14.8 36.0 %copy-start.2 = (bf16[1,512,512]{2,1,0:T(8,128)(2,1)S(1)}, bf16[1,512,512]{2,1,0:T(8,128)(2,1)}, u32[]{:S(2)}) copy-start(bf16[1,512,512]{2,1,0:T(8,128)(2,1)} %param.12) | copy-start | bytes 1572868
  49.8 1.0 copy-start

commit v3 on v2

--- a/solution.py
+++ b/solution.py
@@ -286,7 +286,7 @@
 
 
 def scatter_kernel(
-    waves, place_ref, term_ref, obj_ref, probe_ref, buf, land, cross, other, send, recv, csend, crecv
+    waves, place_ref, obj_ref, buf, land, cross, send, recv, csend, crecv
 ):
     bits = bit_count(waves)
     ring = Halving(waves, buf, land, send, recv)
@@ -301,8 +301,7 @@
 
     lanes = place_ref.shape[1]
     swaps = [to_core(place_ref.at[1 - mine, lane], cross.at[lane], lane) for lane in range(lanes)]
-    terms = [to_core(term_ref.at[c], other.at[c], lanes + c) for c in range(2)]
-    copies = swaps + terms
+    copies = list(swaps)
     for copy in copies:
         copy.start()
     flying = {}
@@ -318,9 +317,6 @@
         copy.start()
         flying[lane] = copy
         copies.append(copy)
-    for c in range(2):
-        terms[c].wait_recv()
-        probe_ref[c] = term_ref[c] + other[c]
     wide = buf.shape[3]
     for lane in range(lanes):
         flying[lane].wait_recv()
@@ -388,22 +384,22 @@
         compiler_params=plain,
         name="backward",
     )(offsets, det, total, measured[0], dense, patch, probe, left, right)
-    object_grad, probe_grad = pl.pallas_call(
+    probe_grad = lax.psum(term, "pos")
+    object_grad = pl.pallas_call(
         functools.partial(scatter_kernel, waves),
-        out_shape=(shape((2, tall, obj_side), F32), shape((2, side, side), F32)),
-        in_specs=[vmem] * 2,
-        out_specs=(vmem,) * 2,
+        out_shape=shape((2, tall, obj_side), F32),
+        in_specs=[vmem],
+        out_specs=vmem,
         scratch_shapes=[
             pltpu.VMEM(place_shape, F32), pltpu.VMEM(place_shape, F32), pltpu.VMEM(place_shape, F32),
-            pltpu.VMEM((2, side, side), F32),
             pltpu.SemaphoreType.DMA((lanes, bits)), pltpu.SemaphoreType.DMA((lanes, bits)),
-            pltpu.SemaphoreType.DMA((lanes + 2,)), pltpu.SemaphoreType.DMA((lanes + 2,)),
+            pltpu.SemaphoreType.DMA((lanes,)), pltpu.SemaphoreType.DMA((lanes,)),
         ],
         compiler_params=pltpu.CompilerParams(
             vmem_limit_bytes=VMEM_BYTES, collective_id=1, has_side_effects=True
         ),
         name="object_sum",
-    )(place, term)
+    )(place)
     return object_grad, probe_grad[None]
 
 

time: 106 us -> 117 us (1.10)
  between operations: 0.66 us -> 14.1 us
  Pallas kernels: 97 us -> 94.8 us
    pallas_call x1, Pallas kernels: 38.3 us -> 36.2 us  [local(): pl.pallas_call(functools.partial(scatter_kernel, waves), out_shape=shape(...]
  transfers between devices with their start and end apart: 0 -> 1, of which waited for: 0 -> 0; matrix products, arithmetic and copies ran while one was open for 0% -> 0% of each run, Pallas kernels for 0% -> 31%
where the time goes in v3:
time: 117 us
  Pallas kernels  94.8 us (81%)
  between operations  14.1 us (12%)
  local copies, waits for them, and re-layouts  8.05 us (7%)
    pallas_call x1, Pallas kernels, local(): pl.pallas_call(functools.partial(scatter_kernel, waves), out_shape=shape(...  36.2 us
    pallas_call x1, Pallas kernels, local(): pl.pallas_call(functools.partial(sum_kernel, waves), out_shape=shape(lane...  35 us
    pallas_call x1, Pallas kernels, local(): pl.pallas_call(functools.partial(backward_kernel, waves), out_shape=(shap...  12.8 us
    pallas_call x1, Pallas kernels, local(): pl.pallas_call(functools.partial(forward_kernel, waves), out_shape=(shape...  10.9 us
    unnamed x13, local copies, waits for them, and re-layouts  8.05 us
  transfers between devices with their start and end apart: 1, of which 0 were waited for; matrix products, arithmetic and copies ran while one was open for 0% of the time, Pallas kernels for 31%

profile of v3, /device:TPU:0, one launch (start us, length us, event | category | flops | bytes accessed | tf_op | source)
XLA Modules:
  0.0 117.0 jit_solution(17425849568110403794)
XLA Ops:
  7.2 0.0 all-reduce.2.cloned.1.call-start
  7.2 0.7 copy.11.off_ref
  8.0 0.0 copy-start.3
  8.0 0.9 copy-done.3
  8.9 0.0 copy-start.4
  8.9 0.7 copy-done.4
  9.5 10.9 %forward.1 = (f32[2,512,512]{2,1,0:T(8,128)}, f32[1024,512]{1,0:T(8,128)}, bf16[512,512]{1,0:T(8,128)(2,1)S(1)}, f32[8,8,32,128]{3,2,1,0:T(8,128)S(1)}) custom-call(s32[2,1]{1,0:T(2,128)S(1)} %copy.11.off_ref, s32[1,8]{1,0:T(1,128)S(1)} %copy-done.4, f32[2,768,768]{2,1,0:T(8,128)} %obj_ref.1, f32[2,512,512]{2,1,0:T(8,128)} %bitcast.6, ...), custom_call_target="tpu_custom_call" | custom-call | tf_op jit(solution)/shard_map/forward/pallas_call | solution.py:340
  20.4 0.0 copy-start.1
  20.4 1.0 copy-done.1
  21.4 0.0 copy-start.2
  21.4 35.0 %intensity_sum.1.total_ref = f32[8,8,32,128]{3,2,1,0:T(8,128)S(1)} custom-call(f32[8,8,32,128]{3,2,1,0:T(8,128)} %copy-done.1), custom_call_target="tpu_custom_call" | custom-call | tf_op jit(solution)/shard_map/intensity_sum/pallas_call | solution.py:355
  56.3 0.0 copy-start
  56.3 1.0 copy-done
  57.3 0.0 copy-done.2
  57.3 12.8 %backward.1 = (f32[2,512,512]{2,1,0:T(8,128)}, f32[2,12,8,48,128]{4,3,2,1,0:T(8,128)}) custom-call(s32[2,1]{1,0:T(2,128)S(1)} %copy.11.off_ref, f32[1024,512]{1,0:T(8,128)} %get-tuple-element.8.det_ref, f32[8,8,32,128]{3,2,1,0:T(8,128)} %copy-done, bf16[512,512]{1,0:T(8,128)(2,1)S(1)} %bitcast.4, bf16[512,512]{1,0:T(8,128)(2,1)S(1)} %get-tuple-element.10.map_ref, ...), custom_call_target="tpu_custom_call" | custom-call | tf_op jit(solution)/shard_map/backward/pallas_call | solution.py:374
  70.2 0.0 all-reduce.2.cloned.1.call-update
  70.2 36.2 %object_sum.1 = f32[2,48,768]{2,1,0:T(8,128)S(1)} custom-call(f32[2,12,8,48,128]{4,3,2,1,0:T(8,128)} %get-tuple-element.12.place_ref), custom_call_target="tpu_custom_call" | custom-call | tf_op jit(solution)/shard_map/object_sum/pallas_call | solution.py:388
  106.4 0.0 all-reduce.2.cloned.1.call-done
  106.4 0.7 copy.14
  107.1 3.1 %copy.15 = f32[1,2,512,512]{3,2,1,0:T(8,128)} copy(f32[1,2,512,512]{3,2,1,0:T(8,128)} %all-reduce.2.cloned.1.call-done) | data formatting | bytes 4194304
Async XLA Ops:
  7.2 99.2 %all-reduce.2.cloned.1.call-start = ((), (), s32[]{:S(2)}) async-start(), calls=%async_computation | async-start | bytes 4194304 | tf_op jit(solution)/shard_map/psum | solution.py:387
  8.0 0.9 copy-start.3
  8.9 0.7 copy-start.4
  20.4 1.0 copy-start.1
  21.4 36.0 %copy-start.2 = (bf16[1,512,512]{2,1,0:T(8,128)(2,1)S(1)}, bf16[1,512,512]{2,1,0:T(8,128)(2,1)}, u32[]{:S(2)}) copy-start(bf16[1,512,512]{2,1,0:T(8,128)(2,1)} %param.12) | copy-start | bytes 1572868
  56.3 1.0 copy-start
Sparse Core Ops, SparseCore 0:
  70.3 20.2 all-reduce.1
